TPU v7x, 256 devices: a whole 4x4x8 slice. The times are simulated.
256 devices in a mesh: gx: 4 (over z_lo), gy: 8 (over x, core), gz: 8 (over z_hi, y).
Axes of the slice: x: 4, y: 4, z: 8 (z_hi: 2, z_lo: 4; z = z_hi * 4 + z_lo), core: 2. Of those that a mesh axis runs over, the one named last changes fastest.
Arguments:
- tokens: bfloat16 [512, 12288], P('gz', 'gx'), may hold values from -6 to 6
- grad_out: bfloat16 [512, 12288], P('gz', 'gx'), may hold values from -6 to 6
- w_in: bfloat16 [12288, 24576], P('gx', ('gy', 'gz')), may hold values from -0.0546875 to 0.0546875
- w_out: bfloat16 [24576, 12288], P(('gy', 'gz'), 'gx'), may hold values from -0.0546875 to 0.0546875
Outputs:
- grad_tokens: bfloat16 [512, 12288], P(('gy', 'gz'), 'gx')
- grad_w_in: bfloat16 [12288, 24576], P('gx', ('gy', 'gz'))
- grad_w_out: bfloat16 [24576, 12288], P(('gy', 'gz'), 'gx')
All inputs are finite; a program needn't handle non-finite values.
Results may differ from a plain program's by a relative error of at most 0.0049.
Values may be sent and summed in bfloat16 or wider, within the bound.
A program may use at most 64 MiB of HBM per device.

v0:
```python
import jax
import jax.numpy as jnp
from jax import lax
from jax.sharding import PartitionSpec as P

coef = 0.7978845608028654


def gelu_pair(pre, back):
    inner = coef * (pre + 0.044715 * pre * pre * pre)
    tval = jnp.tanh(inner)
    act = 0.5 * pre * (1.0 + tval)
    slope = 0.5 * (1.0 + tval) + 0.5 * pre * (1.0 - tval * tval) * coef * (
        1.0 + 3.0 * 0.044715 * pre * pre
    )
    return (act.astype(jnp.bfloat16), (back * slope).astype(jnp.bfloat16))


def shards(tokens, grad_out, w_in, w_out):
    whole_x, whole_dy = (
        lax.all_gather(tokens, "gz", axis=0, tiled=True),
        lax.all_gather(grad_out, "gz", axis=0, tiled=True),
    )
    pre_part = jnp.dot(whole_x, w_in, preferred_element_type=jnp.float32)
    back_part = lax.dot_general(
        whole_dy, w_out, (((1,), (1,)), ((), ())), preferred_element_type=jnp.float32
    )
    pre, back = lax.psum((pre_part, back_part), "gx")
    act, dpre = gelu_pair(pre, back)
    grad_w_out = lax.dot_general(
        act, whole_dy, (((0,), (0,)), ((), ())), preferred_element_type=jnp.float32
    ).astype(jnp.bfloat16)
    grad_w_in = lax.dot_general(
        whole_x, dpre, (((0,), (0,)), ((), ())), preferred_element_type=jnp.float32
    ).astype(jnp.bfloat16)
    grad_tokens = lax.psum_scatter(
        lax.dot_general(dpre, w_in, (((1,), (1,)), ((), ())), preferred_element_type=jnp.float32),
        ("gy", "gz"),
        scatter_dimension=0,
        tiled=True,
    )
    return (grad_tokens.astype(jnp.bfloat16), grad_w_in, grad_w_out)


def solution(mesh):
    placed = (P("gz", "gx"), P("gz", "gx"), P("gx", ("gy", "gz")), P(("gy", "gz"), "gx"))
    return jax.shard_map(
        shards,
        mesh=mesh,
        in_specs=placed,
        out_specs=(P(("gy", "gz"), "gx"), P("gx", ("gy", "gz")), P(("gy", "gz"), "gx")),
        check_vma=False,
    )
```

profile of v0, /device:TPU:1, one launch (start us, length us, event | category | flops | bytes accessed | tf_op | source)
XLA Modules:
  0.0 470.8 jit_solution(17519826866845429790)
XLA Ops:
  7.2 0.0 copy-start
  7.2 0.0 all-gather.3.cloned.1.call-start
  7.2 0.7 all-gather.3.cloned.1.call-update
  7.9 0.0 all-gather.5.cloned.1.call-start
  8.0 0.7 all-gather.5.cloned.1.call-update
  8.7 0.0 all-reduce.3.cloned.1.call-start
  8.7 97.2 %all-gather.3.cloned.1.call-done = bf16[512,3072]{1,0:T(8,128)(2,1)} async-done(((bf16[64,3072]{1,0:T(8,128)(2,1)}), bf16[512,3072]{1,0:T(8,128)(2,1)}) %all-gather.3.cloned.1.call-update) | async-done | bytes 3145744 | tf_op jit(solution)/shard_map/all_gather | solution.py:22
  105.9 5.3 %fusion.16 = f32[512,384]{1,0:T(8,128)} fusion(bf16[512,3072]{1,0:T(8,128)(2,1)} %all-gather.3.cloned.1.call-done, bf16[384,3072]{1,0:T(8,128)(2,1)} %param.7), kind=kOutput, calls=%fused_computation.21 | convolution fusion | flops 1207959552 | bytes 6291456 | tf_op jit(solution)/shard_map/dot_general | solution.py:25
  111.2 84.4 %all-gather.5.cloned.1.call-done = bf16[512,3072]{1,0:T(8,128)(2,1)} async-done(((bf16[64,3072]{1,0:T(8,128)(2,1)}), bf16[512,3072]{1,0:T(8,128)(2,1)}) %all-gather.5.cloned.1.call-update) | async-done | bytes 3145744 | tf_op jit(solution)/shard_map/all_gather | solution.py:21
  195.6 0.0 copy-done
  195.6 4.6 fusion.17
  200.2 0.0 all-reduce.3.cloned.1.call-update
  200.2 0.0 reduce-scatter.2.cloned.1.call-start
  200.2 76.5 %all-reduce.3.cloned.1.call-done = (f32[512,384]{1,0:T(8,128)}, f32[512,384]{1,0:T(8,128)}) async-done(((f32[512,384]{1,0:T(8,128)}, f32[512,384]{1,0:T(8,128)}), (f32[512,384]{1,0:T(8,128)}, f32[512,384]{1,0:T(8,128)})) %all-reduce.3.cloned.1.call-update) | async-done | bytes 1572880 | tf_op jit(solution)/shard_map/psum | solution.py:28
  276.7 1.9 fusion.7
  278.6 4.5 fusion.18
  283.1 0.0 reduce-scatter.2.cloned.1.call-update
  283.1 4.7 %fusion = bf16[3072,384]{0,1:T(8,128)(2,1)} fusion(bf16[512,384]{1,0:T(8,128)(2,1)S(1)} %fusion.7, bf16[512,3072]{1,0:T(8,128)(2,1)} %all-gather.5.cloned.1.call-done), kind=kOutput, calls=%fused_computation.2 | convolution fusion | flops 1209139200 | bytes 5898240 | tf_op jit(solution)/shard_map/dot_general | solution.py:33
  287.8 0.0 copy-start.1
  287.8 4.3 copy.7
  292.2 0.0 copy-done.1
  292.2 4.8 %convolution_convert_fusion = bf16[384,3072]{1,0:T(8,128)(2,1)} fusion(bf16[512,3072]{1,0:T(8,128)(2,1)} %all-gather.3.cloned.1.call-done, f32[512,384]{1,0:T(8,128)S(1)} %copy-done.1), kind=kOutput, calls=%fused_computation | convolution fusion | flops 1210908672 | bytes 6291456 | tf_op jit(solution)/shard_map/dot_general | solution.py:30
  297.0 165.8 %reduce-scatter.2.cloned.1.call-done = f32[8,3072]{1,0:T(8,128)} async-done(((f32[512,3072]{1,0:T(8,128)}), f32[8,3072]{1,0:T(8,128)}) %reduce-scatter.2.cloned.1.call-update) | async-done | bytes 98320 | tf_op jit(solution)/shard_map/reduce_scatter | solution.py:36
  462.8 1.5 convert_element_type.19
Async XLA Ops:
  7.2 188.4 %copy-start = (bf16[3072,384]{1,0:T(8,128)(2,1)S(1)}, bf16[3072,384]{1,0:T(8,128)(2,1)}, u32[]{:S(2)}) copy-start(bf16[3072,384]{1,0:T(8,128)(2,1)} %param.6) | copy-start | bytes 7077892
  7.2 98.7 %all-gather.3.cloned.1.call-start = ((), (), s32[]{:S(2)}) async-start(), calls=%async_computation.1 | async-start | bytes 3538944 | tf_op jit(solution)/shard_map/all_gather | solution.py:22
  7.9 187.7 %all-gather.5.cloned.1.call-start = ((), (), s32[]{:S(2)}) async-start(), calls=%async_computation.2 | async-start | bytes 3538944 | tf_op jit(solution)/shard_map/all_gather | solution.py:21
  8.7 268.0 %all-reduce.3.cloned.1.call-start = ((), (), s32[]{:S(2)}) async-start(), calls=%async_computation.4 | async-start | bytes 3145728 | tf_op jit(solution)/shard_map/psum | solution.py:28
  200.2 262.6 %reduce-scatter.2.cloned.1.call-start = ((), (), s32[]{:S(2)}) async-start(), calls=%async_computation.3 | async-start | bytes 6389760 | tf_op jit(solution)/shard_map/reduce_scatter | solution.py:36
  287.8 4.3 copy-start.1
Sparse Core Ops, SparseCore 0:
  10.6 95.2 all-gather.2
  108.5 87.0 all-gather.4
  200.3 76.3 all-reduce.2
  283.2 179.5 reduce-scatter.1
where the time goes:
time: 472 us; the launch traced here: 471 us
  waiting for transfers between devices  425 us (90%)
  matrix products  23.9 us (5%)
  between operations  13.8 us (3%)
    reduce_scatter x1, waiting for transfers between devices, shards(): lax.psum_scatter(lax.dot_general(dpre, w_in, (((1,), (1,)), ((), ())), pr...  166 us
    all_gather x1, waiting for transfers between devices, shards(): lax.all_gather(grad_out, 'gz', axis=0, tiled=True)  97.2 us
    all_gather x1, waiting for transfers between devices, shards(): lax.all_gather(tokens, 'gz', axis=0, tiled=True)  84.4 us
    psum x1, waiting for transfers between devices, shards(): pre, back = lax.psum((pre_part, back_part), 'gx')  76.5 us
  transfers between devices with their start and end apart: 4, of which 4 were waited for; matrix products, arithmetic and copies ran while one was open for 4% of the time, Pallas kernels for 0%

commit v1 on v0

v1 whole, which is shorter than its diff:
```python
import functools

import jax
import jax.numpy as jnp
from jax import lax
from jax.experimental import pallas as pl
from jax.experimental.pallas import tpu as pltpu
from jax.sharding import PartitionSpec as P

MESH = pl.DeviceIdType.MESH
F32, BF16 = jnp.float32, jnp.bfloat16
coef = 0.7978845608028654
NN = (((1,), (0,)), ((), ()))
NT = (((1,), (1,)), ((), ()))
TN = (((0,), (0,)), ((), ()))

FEAT, HID, TOK = 3072, 384, 512
HALF = FEAT // 2
P2O, P2P = 512, 768
N_SEMS = 128


def gelu_pair(pre, back):
    inner = coef * (pre + 0.044715 * pre * pre * pre)
    tval = jnp.tanh(inner)
    act = 0.5 * pre * (1.0 + tval)
    slope = 0.5 * (1.0 + tval) + 0.5 * pre * (1.0 - tval * tval) * coef * (
        1.0 + 3.0 * 0.044715 * pre * pre
    )
    return act.astype(BF16), (back * slope).astype(BF16)


def dot(a, b, dims):
    return lax.dot_general(a, b, dims, preferred_element_type=F32)


def kernel(
    tok_hbm, dy_hbm, win_hbm, wout_hbm,
    gt_ref, gwi_hbm, gwo_hbm,
    both, win, wout, win_sib, part, part16, inbox, acts, dpre_sib,
    quad, ysend, yrecv, xsend, xrecv, own, fin_send, fin_recv, gwi, gwo,
    ssem, rsem, xs_sem, xr_sem, lsem,
):
    gx, gy, gz = lax.axis_index("gx"), lax.axis_index("gy"), lax.axis_index("gz")
    x, c, y, h, l = gy // 2, gy % 2, gz % 4, gz // 4, gx

    def at(x=x, c=c, y=y, h=h, l=l):
        return (l, x * 2 + c, h * 4 + y)

    def turn(v, d):
        return (v + d + 4) % 4

    l1, l2, l3 = l + 1 - 2 * (l % 2), turn(l, 2), 3 - l
    lane = {1: l1, 2: l2, 3: l3}

    mine = pl.multiple_of(gz * 64, 64)
    loads = [
        pltpu.make_async_copy(tok_hbm, both.at[0, pl.ds(mine, 64)], lsem.at[0]),
        pltpu.make_async_copy(dy_hbm, both.at[1, pl.ds(mine, 64)], lsem.at[1]),
        pltpu.make_async_copy(win_hbm, win, lsem.at[2]),
        pltpu.make_async_copy(wout_hbm, wout, lsem.at[3]),
    ]
    for cp in loads:
        cp.start()

    peers = (
        [at(x=turn(x, d)) for d in (1, 2, 3)]
        + [at(y=turn(y, d)) for d in (1, 2, 3)]
        + [at(l=lane[j]) for j in (1, 2, 3)]
        + [at(h=1 - h), at(h=1 - h, c=1 - c), at(c=1 - c)]
    )
    barrier = pltpu.get_barrier_semaphore()
    for peer in peers:
        pl.semaphore_signal(barrier, inc=1, device_id=peer, device_id_type=MESH)
    pl.semaphore_wait(barrier, len(peers))

    sent = []

    def send(src, dst, peer):
        i = len(sent)
        cp = pltpu.make_async_remote_copy(
            src_ref=src, dst_ref=dst, send_sem=ssem.at[i], recv_sem=rsem.at[i],
            device_id=peer, device_id_type=MESH,
        )
        cp.start()
        sent.append(cp)
        return cp

    def share(which, row, rows, col, cols, peer):
        ref = both.at[which, pl.ds(pl.multiple_of(row, 16), rows), pl.ds(pl.multiple_of(col, 128), cols)]
        return send(ref, ref, peer)

    ALL, TK, DY = slice(0, 2), slice(0, 1), slice(1, 2)
    base = c * HALF
    other = 1 - h
    sib = at(c=1 - c)

    def row(yy, hh):
        return (hh * 4 + yy) * 64

    right_x, left_x = at(x=turn(x, 1)), at(x=turn(x, -1))
    right_y, left_y = at(y=turn(y, 1)), at(y=turn(y, -1))
    ym, yp, yo = turn(y, -1), turn(y, 1), turn(y, 2)
    strip = 16 * x

    loads[0].wait()
    loads[1].wait()

    z0 = share(ALL, row(y, h) + strip, 16, base, HALF, at(h=other))

    def y_first(hh, width):
        return (
            share(ALL, row(y, hh) + strip, 16, base + width, HALF - width, right_y),
            share(ALL, row(y, hh) + strip, 16, base + width, HALF - width, left_y),
        )

    def y_block(hh, width):
        return (
            share(ALL, row(y, hh), 64, base, width, right_y),
            share(ALL, row(y, hh), 64, base, width, left_y),
        )

    def x_strip(yy, hh, col, cols):
        r = row(yy, hh) + strip
        return (
            share(ALL, r, 16, base + col, cols, right_x),
            share(ALL, r, 16, base + col, cols, left_x),
        )

    def x_on(yy, hh, col, cols, got):
        got[0].wait_recv()
        a = share(TK, row(yy, hh) + 16 * turn(x, -1), 16, base + col, cols, right_x)
        got[1].wait_recv()
        b = share(DY, row(yy, hh) + 16 * turn(x, 1), 16, base + col, cols, left_x)
        return a, b

    def arrived(pair):
        pair[0].wait_recv()
        pair[1].wait_recv()

    def to_sibling(yy, hh):
        return share(ALL, row(yy, hh), 64, base, HALF, sib)

    def strips_on(hh, width, got):
        got[0].wait_recv()
        a = share(TK, row(ym, hh) + strip, 16, base + width, HALF - width, right_y)
        xa = x_strip(ym, hh, width, HALF - width)
        got[1].wait_recv()
        b = share(DY, row(yp, hh) + strip, 16, base + width, HALF - width, left_y)
        xb = x_strip(yp, hh, width, HALF - width)
        return (a, b), xa, xb

    def blocks_on(hh, width, got):
        got[0].wait_recv()
        a = share(TK, row(ym, hh), 64, base, width, right_y)
        got[1].wait_recv()
        b = share(DY, row(yp, hh), 64, base, width, left_y)
        return a, b

    yb = y_first(h, P2O)
    ya = y_block(h, P2O)

    yb2, xa1, xa2 = strips_on(h, P2O, yb)
    ya2 = blocks_on(h, P2O, ya)
    arrived(yb2)
    xa3 = x_strip(yo, h, P2O, HALF - P2O)
    xf1 = x_on(ym, h, P2O, HALF - P2O, xa1)
    xf2 = x_on(yp, h, P2O, HALF - P2O, xa2)
    z0.wait_recv()
    pb = y_first(other, P2P)
    zx = x_strip(y, other, 0, HALF)
    xf3 = x_on(yo, h, P2O, HALF - P2O, xa3)
    arrived(ya2)
    arrived(xf1)
    sb1 = to_sibling(ym, h)
    arrived(xf2)
    sb2 = to_sibling(yp, h)
    pb2, px1, px2 = strips_on(other, P2P, pb)
    arrived(xf3)
    sb3 = to_sibling(yo, h)
    zxf = x_on(y, other, 0, HALF, zx)
    loads[2].wait()
    ws = send(
        win.at[pl.ds(pl.multiple_of((1 - c) * HALF, 128), HALF)], win_sib, sib
    )
    loads[3].wait()

    def products(slot, hh):
        r = pl.multiple_of(hh * 256, 256)
        pre = jnp.zeros((256, HID), F32)
        back = jnp.zeros((256, HID), F32)
        for k in range(0, FEAT, 768):
            pre += dot(both[0, pl.ds(r, 256), pl.ds(k, 768)], win[pl.ds(k, 768), :], NN)
        part[slot, 0] = pre
        part16[slot, 0] = pre.astype(BF16)
        for k in range(0, FEAT, 768):
            back += dot(both[1, pl.ds(r, 256), pl.ds(k, 768)], wout[:, pl.ds(k, 768)], NT)
        part[slot, 1] = back
        part16[slot, 1] = back.astype(BF16)

    def scatter(slot, s):
        out = {}
        for j in (3, 2, 1):
            src = part16.at[slot, :, pl.ds(pl.multiple_of(s * 128 + 32 * lane[j], 32), 32)]
            out[j] = send(src, inbox.at[slot * 2 + s, j - 1], at(l=lane[j]))
        return out

    sb1.wait_recv()
    sb2.wait_recv()
    sb3.wait_recv()
    products(0, h)
    rs = {0: scatter(0, 0), 1: scatter(0, 1)}

    arrived(pb2)
    px3 = x_strip(yo, other, P2P, HALF - P2P)
    arrived(zxf)
    pa = y_block(other, P2P)
    sp0 = to_sibling(y, other)
    pf1 = x_on(ym, other, P2P, HALF - P2P, px1)
    pf2 = x_on(yp, other, P2P, HALF - P2P, px2)
    pa2 = blocks_on(other, P2P, pa)
    pf3 = x_on(yo, other, P2P, HALF - P2P, px3)
    arrived(pf1)
    sp1 = to_sibling(ym, other)
    arrived(pf2)
    sp2 = to_sibling(yp, other)

    def rows_of(k):
        hh = h if k < 2 else other
        return hh * 256 + (k % 2) * 128

    def finish_sum(k):
        slot, s = k // 2, k % 2
        for j in (1, 2, 3):
            rs[k][j].wait_recv()
        r = pl.multiple_of(s * 128 + 32 * l, 32)
        pre = part[slot, 0, pl.ds(r, 32)]
        back = part[slot, 1, pl.ds(r, 32)]
        for j in (1, 2, 3):
            pre += inbox[k, j - 1, 0].astype(F32)
            back += inbox[k, j - 1, 1].astype(F32)
        act, dpre = gelu_pair(pre, back)
        q = pl.multiple_of(rows_of(k) + 32 * l, 32)
        acts[0, pl.ds(q, 32)] = act
        acts[1, pl.ds(q, 32)] = dpre
        ref = acts.at[:, pl.ds(q, 32)]
        return send(ref, ref, at(l=l2)), send(ref, ref, at(l=l1))

    def pass_on(k, ag):
        ag[0].wait_recv()
        ref = acts.at[:, pl.ds(pl.multiple_of(rows_of(k) + 32 * l2, 32), 32)]
        return send(ref, ref, at(l=l1))

    def to_pair(k, ag, fw):
        ag[1].wait_recv()
        fw.wait_recv()
        r = pl.ds(pl.multiple_of(rows_of(k), 128), 128)
        return send(acts.at[1, r], dpre_sib.at[r], sib)

    def token_part(k, sd):
        sd.wait_recv()
        r = pl.ds(pl.multiple_of(rows_of(k), 128), 128)
        for col in range(0, HALF, 512):
            w = win[pl.ds(pl.multiple_of(base + col, 128), 512), :]
            q = dot(acts[1, r], w, NT) + dot(dpre_sib[r], win_sib[pl.ds(col, 512), :], NT)
            quad[k, :, :, :, pl.ds(col, 512)] = q.reshape(4, 4, 8, 512)
        out = []
        for j in (2, 1, 3):
            yy = turn(y, j)
            ysend[k, j - 1] = quad[k, :, yy].reshape(32, HALF).astype(BF16)
            out.append(send(ysend.at[k, j - 1], yrecv.at[k, j - 1], at(y=yy)))
        return out

    def x_copy(k, xx):
        j = (xx - x + 4) % 4
        return pltpu.make_async_remote_copy(
            src_ref=xsend.at[k], dst_ref=xrecv.at[j - 1],
            send_sem=xs_sem.at[k], recv_sem=xr_sem.at[j - 1],
            device_id=at(x=xx), device_id_type=MESH,
        )

    def x_dest(k):
        return 2 * (h if k < 2 else other) + k % 2

    def y_sum(k, cy):
        for cp in cy:
            cp.wait_recv()
        total = quad[k, :, y].reshape(32, HALF)
        for j in (1, 2, 3):
            total += yrecv[k, j - 1].astype(F32)
        xx = x_dest(k)

        @pl.when(x == xx)
        def _():
            own[...] = total

        @pl.when(x != xx)
        def _():
            xsend[k] = total.astype(BF16)
            x_copy(k, xx).start()

    ag = {0: finish_sum(0)}
    arrived(pa2)
    arrived(pf3)
    sp3 = to_sibling(yo, other)
    for cp in (sp0, sp1, sp2, sp3):
        cp.wait_recv()
    products(1, other)
    rs[2] = scatter(1, 0)
    rs[3] = scatter(1, 1)
    ws.wait_recv()
    ag[1] = finish_sum(1)
    fw = {0: pass_on(0, ag[0])}
    fw[1] = pass_on(1, ag[1])
    sd = {0: to_pair(0, ag[0], fw[0])}
    cy = {0: token_part(0, sd[0])}
    ag[2] = finish_sum(2)
    sd[1] = to_pair(1, ag[1], fw[1])
    cy[1] = token_part(1, sd[1])
    ag[3] = finish_sum(3)
    fw[2] = pass_on(2, ag[2])
    y_sum(0, cy[0])
    fw[3] = pass_on(3, ag[3])
    sd[2] = to_pair(2, ag[2], fw[2])
    cy[2] = token_part(2, sd[2])
    y_sum(1, cy[1])
    sd[3] = to_pair(3, ag[3], fw[3])
    cy[3] = token_part(3, sd[3])

    def grad_out_tile(i, _):
        col = pl.ds(pl.multiple_of(i * 512, 512), 512)
        gwo[:, col] = dot(acts[0], both[1, :, col], TN).astype(BF16)
        return 0

    def grad_in_tile(i, _):
        col = pl.ds(pl.multiple_of(i * 512, 512), 512)
        gwi[col, :] = dot(both[0, :, col], acts[1], TN).astype(BF16)
        return 0

    lax.fori_loop(0, FEAT // 512, grad_out_tile, 0)
    save_o = pltpu.make_async_copy(gwo, gwo_hbm, lsem.at[4])
    save_o.start()
    y_sum(2, cy[2])
    y_sum(3, cy[3])
    lax.fori_loop(0, FEAT // 512, grad_in_tile, 0)
    save_i = pltpu.make_async_copy(gwi, gwi_hbm, lsem.at[5])
    save_i.start()

    total = own[...]
    for j in (1, 2, 3):
        pltpu.make_async_remote_copy(
            src_ref=xsend.at[0], dst_ref=xrecv.at[j - 1], send_sem=xs_sem.at[0],
            recv_sem=xr_sem.at[j - 1], device_id=at(x=turn(x, j)), device_id_type=MESH,
        ).wait_recv()
        total += xrecv[j - 1].astype(F32)
    fin_send[...] = total.reshape(2, 2, 8, HALF)
    f1 = send(fin_send.at[c, other], fin_recv.at[0], at(h=other))
    f2 = send(fin_send.at[1 - c, other], fin_recv.at[1], at(h=other, c=1 - c))
    f3 = send(fin_send.at[1 - c, h], fin_recv.at[2], sib)
    f1.wait_recv()
    gt_ref[:, pl.ds(pl.multiple_of(base, 128), HALF)] = (
        fin_send[c, h] + fin_recv[0]
    ).astype(BF16)
    f2.wait_recv()
    f3.wait_recv()
    gt_ref[:, pl.ds(pl.multiple_of((1 - c) * HALF, 128), HALF)] = (
        fin_recv[1] + fin_recv[2]
    ).astype(BF16)

    for k in range(4):
        xx = x_dest(k)

        @pl.when(x != xx)
        def _():
            x_copy(k, xx).wait_send()

    for cp in sent:
        cp.wait_send()
    save_o.wait()
    save_i.wait()


def shards(tokens, grad_out, w_in, w_out):
    any_ = pl.BlockSpec(memory_space=pl.ANY)
    vm = pltpu.VMEM
    return pl.pallas_call(
        kernel,
        out_shape=(
            jax.ShapeDtypeStruct((8, FEAT), BF16),
            jax.ShapeDtypeStruct((FEAT, HID), BF16),
            jax.ShapeDtypeStruct((HID, FEAT), BF16),
        ),
        in_specs=[any_] * 4,
        out_specs=(pl.BlockSpec(memory_space=pltpu.VMEM), any_, any_),
        scratch_shapes=[
            vm((2, TOK, FEAT), BF16),
            vm((FEAT, HID), BF16),
            vm((HID, FEAT), BF16),
            vm((HALF, HID), BF16),
            vm((2, 2, 256, HID), F32),
            vm((2, 2, 256, HID), BF16),
            vm((4, 3, 2, 32, HID), BF16),
            vm((2, TOK, HID), BF16),
            vm((TOK, HID), BF16),
            vm((4, 4, 4, 8, HALF), F32),
            vm((4, 3, 32, HALF), BF16),
            vm((4, 3, 32, HALF), BF16),
            vm((4, 32, HALF), BF16),
            vm((3, 32, HALF), BF16),
            vm((32, HALF), F32),
            vm((2, 2, 8, HALF), F32),
            vm((3, 8, HALF), F32),
            vm((FEAT, HID), BF16),
            vm((HID, FEAT), BF16),
            pltpu.SemaphoreType.DMA((N_SEMS,)),
            pltpu.SemaphoreType.DMA((N_SEMS,)),
            pltpu.SemaphoreType.DMA((4,)),
            pltpu.SemaphoreType.DMA((3,)),
            pltpu.SemaphoreType.DMA((6,)),
        ],
        compiler_params=pltpu.CompilerParams(
            collective_id=0, has_side_effects=True, vmem_limit_bytes=44 << 20
        ),
        cost_estimate=pl.CostEstimate(
            flops=6_000_000_000, bytes_accessed=12_000_000, transcendentals=100_000
        ),
        name="ffn_backward",
    )(tokens, grad_out, w_in, w_out)


def solution(mesh):
    placed = (P("gz", "gx"), P("gz", "gx"), P("gx", ("gy", "gz")), P(("gy", "gz"), "gx"))
    return jax.shard_map(
        shards,
        mesh=mesh,
        in_specs=placed,
        out_specs=(P(("gy", "gz"), "gx"), P("gx", ("gy", "gz")), P(("gy", "gz"), "gx")),
        check_vma=False,
    )
```

time: 472 us -> 102 us (0.22)
  the two profiles are of different devices: /device:TPU:1 before, /device:TPU:3 now
where the time goes in v1:
time: 102 us
  Pallas kernels  92.7 us (91%)
  local copies, waits for them, and re-layouts  8.75 us (9%)
    pallas_call x1, Pallas kernels, shards(): pl.pallas_call(kernel, out_shape=(jax.ShapeDtypeStruct((8, FEAT), BF16),...  92.7 us
    unnamed x11, local copies, waits for them, and re-layouts  8.75 us

profile of v1, /device:TPU:3, one launch (start us, length us, event | category | flops | bytes accessed | tf_op | source)
XLA Modules:
  0.0 102.1 jit_solution(7380806664461907505)
XLA Ops:
  0.6 0.0 copy-start
  0.6 1.7 %copy-done = bf16[3072,384]{1,0:T(8,128)(2,1)S(1)} copy-done((bf16[3072,384]{1,0:T(8,128)(2,1)S(1)}, bf16[3072,384]{1,0:T(8,128)(2,1)}, u32[]{:S(2)}) %copy-start) | copy-done | bytes 2359320
  2.3 0.0 copy-start.1
  2.3 1.7 %copy-done.1 = bf16[384,3072]{1,0:T(8,128)(2,1)S(1)} copy-done((bf16[384,3072]{1,0:T(8,128)(2,1)S(1)}, bf16[384,3072]{1,0:T(8,128)(2,1)}, u32[]{:S(2)}) %copy-start.1) | copy-done | bytes 2359320
  4.0 0.0 copy-start.2
  4.0 1.0 copy-done.2
  5.0 0.0 copy-start.3
  5.0 1.0 copy-done.3
  6.0 92.7 %ffn_backward.1 = (bf16[8,3072]{1,0:T(8,128)(2,1)S(1)}, bf16[3072,384]{1,0:T(8,128)(2,1)S(1)}, bf16[384,3072]{1,0:T(8,128)(2,1)S(1)}) custom-call(bf16[64,3072]{1,0:T(8,128)(2,1)S(1)} %copy-done.2, bf16[64,3072]{1,0:T(8,128)(2,1)S(1)} %copy-done.3, bf16[3072,384]{1,0:T(8,128)(2,1)S(1)} %copy-done, bf16[384,3072]{1,0:T(8,128)(2,1)S(1)} %copy-done.1), custom_call_target="tpu_custom_call" | custom-call | flops 6000000000 | bytes 12000000 | tf_op jit(solution)/shard_map/ffn_backward/pallas_call | solution.py:386
  98.6 0.6 copy.10
  99.3 1.4 %copy.11 = bf16[3072,384]{1,0:T(8,128)(2,1)} copy(bf16[3072,384]{1,0:T(8,128)(2,1)S(1)} %get-tuple-element.7) | data formatting | bytes 4718592
  100.7 1.4 %copy.12 = bf16[384,3072]{1,0:T(8,128)(2,1)} copy(bf16[384,3072]{1,0:T(8,128)(2,1)S(1)} %get-tuple-element.8) | data formatting | bytes 4718592
Async XLA Ops:
  0.6 1.7 %copy-start = (bf16[3072,384]{1,0:T(8,128)(2,1)S(1)}, bf16[3072,384]{1,0:T(8,128)(2,1)}, u32[]{:S(2)}) copy-start(bf16[3072,384]{1,0:T(8,128)(2,1)} %win_hbm.1) | copy-start | bytes 7077892
  2.3 1.7 %copy-start.1 = (bf16[384,3072]{1,0:T(8,128)(2,1)S(1)}, bf16[384,3072]{1,0:T(8,128)(2,1)}, u32[]{:S(2)}) copy-start(bf16[384,3072]{1,0:T(8,128)(2,1)} %wout_hbm.1) | copy-start | bytes 7077892
  4.0 1.0 copy-start.2
  5.0 1.0 copy-start.3

commit v2 on v1

--- a/solution.py
+++ b/solution.py
@@ -16,7 +16,7 @@
 
 FEAT, HID, TOK = 3072, 384, 512
 HALF = FEAT // 2
-P2O, P2P = 512, 768
+P2O, P2P = 768, 512
 N_SEMS = 128
 
 
@@ -90,7 +90,7 @@
         ref = both.at[which, pl.ds(pl.multiple_of(row, 16), rows), pl.ds(pl.multiple_of(col, 128), cols)]
         return send(ref, ref, peer)
 
-    ALL, TK, DY = slice(0, 2), slice(0, 1), slice(1, 2)
+    ALL = slice(0, 2)
     base = c * HALF
     other = 1 - h
     sib = at(c=1 - c)
@@ -98,162 +98,157 @@
     def row(yy, hh):
         return (hh * 4 + yy) * 64
 
-    right_x, left_x = at(x=turn(x, 1)), at(x=turn(x, -1))
-    right_y, left_y = at(y=turn(y, 1)), at(y=turn(y, -1))
-    ym, yp, yo = turn(y, -1), turn(y, 1), turn(y, 2)
     strip = 16 * x
 
     loads[0].wait()
     loads[1].wait()
 
+    turns = (1, 3, 2)
     z0 = share(ALL, row(y, h) + strip, 16, base, HALF, at(h=other))
 
-    def y_first(hh, width):
-        return (
-            share(ALL, row(y, hh) + strip, 16, base + width, HALF - width, right_y),
-            share(ALL, row(y, hh) + strip, 16, base + width, HALF - width, left_y),
-        )
-
-    def y_block(hh, width):
-        return (
-            share(ALL, row(y, hh), 64, base, width, right_y),
-            share(ALL, row(y, hh), 64, base, width, left_y),
-        )
-
-    def x_strip(yy, hh, col, cols):
+    def to_y(hh, first, rows, col, cols):
+        return {
+            j: share(ALL, row(y, hh) + first, rows, base + col, cols, at(y=turn(y, j)))
+            for j in turns
+        }
+
+    def to_x(yy, hh, col, cols):
         r = row(yy, hh) + strip
-        return (
-            share(ALL, r, 16, base + col, cols, right_x),
-            share(ALL, r, 16, base + col, cols, left_x),
-        )
-
-    def x_on(yy, hh, col, cols, got):
-        got[0].wait_recv()
-        a = share(TK, row(yy, hh) + 16 * turn(x, -1), 16, base + col, cols, right_x)
-        got[1].wait_recv()
-        b = share(DY, row(yy, hh) + 16 * turn(x, 1), 16, base + col, cols, left_x)
-        return a, b
-
-    def arrived(pair):
-        pair[0].wait_recv()
-        pair[1].wait_recv()
-
-    def to_sibling(yy, hh):
-        return share(ALL, row(yy, hh), 64, base, HALF, sib)
+        return [share(ALL, r, 16, base + col, cols, at(x=turn(x, j))) for j in turns]
 
     def strips_on(hh, width, got):
-        got[0].wait_recv()
-        a = share(TK, row(ym, hh) + strip, 16, base + width, HALF - width, right_y)
-        xa = x_strip(ym, hh, width, HALF - width)
-        got[1].wait_recv()
-        b = share(DY, row(yp, hh) + strip, 16, base + width, HALF - width, left_y)
-        xb = x_strip(yp, hh, width, HALF - width)
-        return (a, b), xa, xb
-
-    def blocks_on(hh, width, got):
-        got[0].wait_recv()
-        a = share(TK, row(ym, hh), 64, base, width, right_y)
-        got[1].wait_recv()
-        b = share(DY, row(yp, hh), 64, base, width, left_y)
-        return a, b
-
-    yb = y_first(h, P2O)
-    ya = y_block(h, P2O)
-
-    yb2, xa1, xa2 = strips_on(h, P2O, yb)
-    ya2 = blocks_on(h, P2O, ya)
-    arrived(yb2)
-    xa3 = x_strip(yo, h, P2O, HALF - P2O)
-    xf1 = x_on(ym, h, P2O, HALF - P2O, xa1)
-    xf2 = x_on(yp, h, P2O, HALF - P2O, xa2)
+        out = {}
+        for j in turns:
+            got[j].wait_recv()
+            out[j] = to_x(turn(y, -j), hh, width, HALF - width)
+        return out
+
+    def to_sibling(yy, hh, col, cols):
+        return share(ALL, row(yy, hh), 64, base + col, cols, sib)
+
+    def arrived(copies):
+        for cp in copies:
+            cp.wait_recv()
+
+    def products(pos, pieces):
+        n = sum(rows for _, rows in pieces)
+        for which, w, dims in ((0, win, NN), (1, wout, NT)):
+            total = jnp.zeros((n, HID), F32)
+            for k in range(0, FEAT, 768):
+                lhs = [
+                    both[which, pl.ds(pl.multiple_of(r, 64), rows), pl.ds(k, 768)]
+                    for r, rows in pieces
+                ]
+                lhs = lhs[0] if len(lhs) == 1 else jnp.concatenate(lhs, axis=0)
+                rhs = w[pl.ds(k, 768), :] if which == 0 else w[:, pl.ds(k, 768)]
+                total += dot(lhs, rhs, dims)
+            part[which, pl.ds(pos, n)] = total
+            part16[which, pl.ds(pos, n)] = total.astype(BF16)
+
+    chunks = [
+        (0, 16, lambda v: row(y, h) + 16 * v),
+        (64, 32, lambda v: row(turn(y, 2 * (v // 2) - 1), h) + 32 * (v % 2)),
+        (192, 16, lambda v: row(turn(y, 2), h) + 16 * v),
+        (256, 32, lambda v: row(0, other) + 32 * v),
+        (384, 32, lambda v: row(2, other) + 32 * v),
+    ]
+
+    def scatter(k):
+        pos, m, _ = chunks[k]
+        out = []
+        for j in (3, 2, 1):
+            src = part16.at[:, pl.ds(pl.multiple_of(pos + m * lane[j], 16), m)]
+            out.append(send(src, inbox.at[k, j - 1, :, pl.ds(0, m)], at(l=lane[j])))
+        return out
+
+    def share_rows(k, v):
+        _, m, first = chunks[k]
+        return pl.ds(pl.multiple_of(first(v), 16), m)
+
+    def finish_sum(k):
+        pos, m, _ = chunks[k]
+        for cp in rs[k]:
+            cp.wait_recv()
+        r = pl.ds(pl.multiple_of(pos + m * l, 16), m)
+        pre, back = part[0, r], part[1, r]
+        for j in (1, 2, 3):
+            pre += inbox[k, j - 1, 0, 0:m].astype(F32)
+            back += inbox[k, j - 1, 1, 0:m].astype(F32)
+        act, dpre = gelu_pair(pre, back)
+        q = share_rows(k, l)
+        acts[0, q] = act
+        acts[1, q] = dpre
+        ref = acts.at[:, q]
+        ag[k] = [send(ref, ref, at(l=l2)), send(ref, ref, at(l=l1))]
+
+    def pass_on(k):
+        ag[k][0].wait_recv()
+        ref = acts.at[:, share_rows(k, l2)]
+        ag[k].append(send(ref, ref, at(l=l1)))
+
+    def gathered(k):
+        ag[k][1].wait_recv()
+        ag[k][2].wait_recv()
+
+    rs, ag = {}, {}
+    yb = to_y(h, strip, 16, P2O, HALF - P2O)
+    ya = to_y(h, 0, 64, 0, P2O)
+    loads[2].wait()
+    loads[3].wait()
+    products(0, [(row(y, h), 64)])
+    rs[0] = scatter(0)
+    xa = strips_on(h, P2O, yb)
     z0.wait_recv()
-    pb = y_first(other, P2P)
-    zx = x_strip(y, other, 0, HALF)
-    xf3 = x_on(yo, h, P2O, HALF - P2O, xa3)
-    arrived(ya2)
-    arrived(xf1)
-    sb1 = to_sibling(ym, h)
-    arrived(xf2)
-    sb2 = to_sibling(yp, h)
-    pb2, px1, px2 = strips_on(other, P2P, pb)
-    arrived(xf3)
-    sb3 = to_sibling(yo, h)
-    zxf = x_on(y, other, 0, HALF, zx)
-    loads[2].wait()
+    zx = to_x(y, other, 0, HALF)
+    pb = to_y(other, strip, 16, P2P, HALF - P2P)
+    finish_sum(0)
     ws = send(
         win.at[pl.ds(pl.multiple_of((1 - c) * HALF, 128), HALF)], win_sib, sib
     )
-    loads[3].wait()
-
-    def products(slot, hh):
-        r = pl.multiple_of(hh * 256, 256)
-        pre = jnp.zeros((256, HID), F32)
-        back = jnp.zeros((256, HID), F32)
-        for k in range(0, FEAT, 768):
-            pre += dot(both[0, pl.ds(r, 256), pl.ds(k, 768)], win[pl.ds(k, 768), :], NN)
-        part[slot, 0] = pre
-        part16[slot, 0] = pre.astype(BF16)
-        for k in range(0, FEAT, 768):
-            back += dot(both[1, pl.ds(r, 256), pl.ds(k, 768)], wout[:, pl.ds(k, 768)], NT)
-        part[slot, 1] = back
-        part16[slot, 1] = back.astype(BF16)
-
-    def scatter(slot, s):
-        out = {}
-        for j in (3, 2, 1):
-            src = part16.at[slot, :, pl.ds(pl.multiple_of(s * 128 + 32 * lane[j], 32), 32)]
-            out[j] = send(src, inbox.at[slot * 2 + s, j - 1], at(l=lane[j]))
-        return out
-
-    sb1.wait_recv()
-    sb2.wait_recv()
-    sb3.wait_recv()
-    products(0, h)
-    rs = {0: scatter(0, 0), 1: scatter(0, 1)}
-
-    arrived(pb2)
-    px3 = x_strip(yo, other, P2P, HALF - P2P)
-    arrived(zxf)
-    pa = y_block(other, P2P)
-    sp0 = to_sibling(y, other)
-    pf1 = x_on(ym, other, P2P, HALF - P2P, px1)
-    pf2 = x_on(yp, other, P2P, HALF - P2P, px2)
-    pa2 = blocks_on(other, P2P, pa)
-    pf3 = x_on(yo, other, P2P, HALF - P2P, px3)
-    arrived(pf1)
-    sp1 = to_sibling(ym, other)
-    arrived(pf2)
-    sp2 = to_sibling(yp, other)
+    got = []
+    for j in (1, 3):
+        ya[j].wait_recv()
+        got.append(to_sibling(turn(y, -j), h, 0, P2O))
+    for j in (1, 3):
+        arrived(xa[j])
+        got.append(to_sibling(turn(y, -j), h, P2O, HALF - P2O))
+    pass_on(0)
+    arrived(got)
+    products(64, [(row(turn(y, -1), h), 64), (row(turn(y, 1), h), 64)])
+    rs[1] = scatter(1)
+    ya[2].wait_recv()
+    got = [to_sibling(turn(y, 2), h, 0, P2O)]
+    arrived(xa[2])
+    got.append(to_sibling(turn(y, 2), h, P2O, HALF - P2O))
+    px = strips_on(other, P2P, pb)
+    arrived(got)
+    products(192, [(row(turn(y, 2), h), 64)])
+    rs[2] = scatter(2)
+    arrived(zx)
+    pa = to_y(other, 0, 64, 0, P2P)
+    got = [to_sibling(y, other, 0, HALF)]
+    finish_sum(1)
+    gathered(0)
+    for j in turns:
+        arrived(px[j])
+        got.append(to_sibling(turn(y, -j), other, P2P, HALF - P2P))
+    finish_sum(2)
+    pass_on(1)
+    for j in turns:
+        pa[j].wait_recv()
+        got.append(to_sibling(turn(y, -j), other, 0, P2P))
+    arrived(got)
+    products(256, [(row(0, other), 256)])
+    rs[3] = scatter(3)
+    rs[4] = scatter(4)
+    pass_on(2)
+    ws.wait_recv()
 
     def rows_of(k):
         hh = h if k < 2 else other
         return hh * 256 + (k % 2) * 128
 
-    def finish_sum(k):
-        slot, s = k // 2, k % 2
-        for j in (1, 2, 3):
-            rs[k][j].wait_recv()
-        r = pl.multiple_of(s * 128 + 32 * l, 32)
-        pre = part[slot, 0, pl.ds(r, 32)]
-        back = part[slot, 1, pl.ds(r, 32)]
-        for j in (1, 2, 3):
-            pre += inbox[k, j - 1, 0].astype(F32)
-            back += inbox[k, j - 1, 1].astype(F32)
-        act, dpre = gelu_pair(pre, back)
-        q = pl.multiple_of(rows_of(k) + 32 * l, 32)
-        acts[0, pl.ds(q, 32)] = act
-        acts[1, pl.ds(q, 32)] = dpre
-        ref = acts.at[:, pl.ds(q, 32)]
-        return send(ref, ref, at(l=l2)), send(ref, ref, at(l=l1))
-
-    def pass_on(k, ag):
-        ag[0].wait_recv()
-        ref = acts.at[:, pl.ds(pl.multiple_of(rows_of(k) + 32 * l2, 32), 32)]
-        return send(ref, ref, at(l=l1))
-
-    def to_pair(k, ag, fw):
-        ag[1].wait_recv()
-        fw.wait_recv()
+    def to_pair(k):
         r = pl.ds(pl.multiple_of(rows_of(k), 128), 128)
         return send(acts.at[1, r], dpre_sib.at[r], sib)
 
@@ -299,32 +294,22 @@
             xsend[k] = total.astype(BF16)
             x_copy(k, xx).start()
 
-    ag = {0: finish_sum(0)}
-    arrived(pa2)
-    arrived(pf3)
-    sp3 = to_sibling(yo, other)
-    for cp in (sp0, sp1, sp2, sp3):
-        cp.wait_recv()
-    products(1, other)
-    rs[2] = scatter(1, 0)
-    rs[3] = scatter(1, 1)
-    ws.wait_recv()
-    ag[1] = finish_sum(1)
-    fw = {0: pass_on(0, ag[0])}
-    fw[1] = pass_on(1, ag[1])
-    sd = {0: to_pair(0, ag[0], fw[0])}
+    gathered(1)
+    gathered(2)
+    sd = {0: to_pair(0), 1: to_pair(1)}
     cy = {0: token_part(0, sd[0])}
-    ag[2] = finish_sum(2)
-    sd[1] = to_pair(1, ag[1], fw[1])
     cy[1] = token_part(1, sd[1])
-    ag[3] = finish_sum(3)
-    fw[2] = pass_on(2, ag[2])
+    finish_sum(3)
+    pass_on(3)
+    finish_sum(4)
     y_sum(0, cy[0])
-    fw[3] = pass_on(3, ag[3])
-    sd[2] = to_pair(2, ag[2], fw[2])
+    y_sum(1, cy[1])
+    gathered(3)
+    sd[2] = to_pair(2)
+    pass_on(4)
     cy[2] = token_part(2, sd[2])
-    y_sum(1, cy[1])
-    sd[3] = to_pair(3, ag[3], fw[3])
+    gathered(4)
+    sd[3] = to_pair(3)
     cy[3] = token_part(3, sd[3])
 
     def grad_out_tile(i, _):
@@ -397,9 +382,9 @@
             vm((FEAT, HID), BF16),
             vm((HID, FEAT), BF16),
             vm((HALF, HID), BF16),
-            vm((2, 2, 256, HID), F32),
-            vm((2, 2, 256, HID), BF16),
-            vm((4, 3, 2, 32, HID), BF16),
+            vm((2, TOK, HID), F32),
+            vm((2, TOK, HID), BF16),
+            vm((5, 3, 2, 32, HID), BF16),
             vm((2, TOK, HID), BF16),
             vm((TOK, HID), BF16),
             vm((4, 4, 4, 8, HALF), F32),
@@ -419,7 +404,7 @@
             pltpu.SemaphoreType.DMA((6,)),
         ],
         compiler_params=pltpu.CompilerParams(
-            collective_id=0, has_side_effects=True, vmem_limit_bytes=44 << 20
+            collective_id=0, has_side_effects=True, vmem_limit_bytes=56 << 20
         ),
         cost_estimate=pl.CostEstimate(
             flops=6_000_000_000, bytes_accessed=12_000_000, transcendentals=100_000

time: 102 us -> 94.6 us (0.927)
  the two profiles are of different devices: /device:TPU:3 before, /device:TPU:35 now
where the time goes in v2:
time: 94.6 us; the launch traced here: 94.5 us
  Pallas kernels  87.5 us (92%)
  local copies, waits for them, and re-layouts  6.29 us (7%)
    pallas_call x1, Pallas kernels, shards(): pl.pallas_call(kernel, out_shape=(jax.ShapeDtypeStruct((8, FEAT), BF16),...  87.5 us
    unnamed x5, local copies, waits for them, and re-layouts  6.29 us

profile of v2, /device:TPU:35, one launch (start us, length us, event | category | flops | bytes accessed | tf_op | source)
XLA Modules:
  0.0 94.5 jit_solution(17574481272430671678)
XLA Ops:
  0.6 87.5 %ffn_backward.1 = (bf16[8,3072]{1,0:T(8,128)(2,1)}, bf16[3072,384]{1,0:T(8,128)(2,1)}, bf16[384,3072]{1,0:T(8,128)(2,1)}) custom-call(bf16[64,3072]{1,0:T(8,128)(2,1)} %tok_hbm.1, bf16[64,3072]{1,0:T(8,128)(2,1)} %dy_hbm.1, bf16[3072,384]{1,0:T(8,128)(2,1)} %win_hbm.1, bf16[384,3072]{1,0:T(8,128)(2,1)} %wout_hbm.1), custom_call_target="tpu_custom_call" | custom-call | flops 6000000000 | bytes 12000000 | tf_op jit(solution)/shard_map/ffn_backward/pallas_call | solution.py:371
  88.2 1.4 %copy.10 = bf16[8,3072]{1,0:T(8,128)(2,1)} copy(bf16[8,3072]{1,0:T(8,128)(2,1)} %get-tuple-element.6) | data formatting | bytes 98304
  89.6 0.0 copy-start
  89.6 3.5 %copy.11 = bf16[3072,384]{1,0:T(8,128)(2,1)} copy(bf16[3072,384]{1,0:T(8,128)(2,1)} %get-tuple-element.7) | data formatting | bytes 4718592
  93.0 0.0 copy-done
  93.1 1.4 %copy.12 = bf16[384,3072]{1,0:T(8,128)(2,1)} copy(bf16[384,3072]{1,0:T(8,128)(2,1)S(1)} %copy-done) | data formatting | bytes 4718592
Async XLA Ops:
  89.6 3.5 %copy-start = (bf16[384,3072]{1,0:T(8,128)(2,1)S(1)}, bf16[384,3072]{1,0:T(8,128)(2,1)}, u32[]{:S(2)}) copy-start(bf16[384,3072]{1,0:T(8,128)(2,1)} %get-tuple-element.8) | copy-start | bytes 7077892

commit v3 on v2

--- a/solution.py
+++ b/solution.py
@@ -39,7 +39,7 @@
     gt_ref, gwi_hbm, gwo_hbm,
     both, win, wout, win_sib, part, part16, inbox, acts, dpre_sib,
     quad, ysend, yrecv, xsend, xrecv, own, fin_send, fin_recv, gwi, gwo,
-    ssem, rsem, xs_sem, xr_sem, lsem,
+    ssem, rsem, xs_sem, xr_sem, fs_sem, fr_sem, lsem,
 ):
     gx, gy, gz = lax.axis_index("gx"), lax.axis_index("gy"), lax.axis_index("gz")
     x, c, y, h, l = gy // 2, gy % 2, gz % 4, gz // 4, gx
@@ -149,8 +149,8 @@
         (0, 16, lambda v: row(y, h) + 16 * v),
         (64, 32, lambda v: row(turn(y, 2 * (v // 2) - 1), h) + 32 * (v % 2)),
         (192, 16, lambda v: row(turn(y, 2), h) + 16 * v),
-        (256, 32, lambda v: row(0, other) + 32 * v),
-        (384, 32, lambda v: row(2, other) + 32 * v),
+        (256, 32, lambda v: row(2 * (v // 2), other) + 32 * (v % 2)),
+        (384, 32, lambda v: row(2 * (v // 2) + 1, other) + 32 * (v % 2)),
     ]
 
     def scatter(k):
@@ -232,32 +232,37 @@
     for j in turns:
         arrived(px[j])
         got.append(to_sibling(turn(y, -j), other, P2P, HALF - P2P))
-    finish_sum(2)
-    pass_on(1)
     for j in turns:
         pa[j].wait_recv()
         got.append(to_sibling(turn(y, -j), other, 0, P2P))
+    finish_sum(2)
+    pass_on(1)
     arrived(got)
-    products(256, [(row(0, other), 256)])
+    products(256, [(row(b, other), 64) for b in (0, 2, 1, 3)])
     rs[3] = scatter(3)
     rs[4] = scatter(4)
     pass_on(2)
+    gathered(1)
     ws.wait_recv()
 
-    def rows_of(k):
-        hh = h if k < 2 else other
-        return hh * 256 + (k % 2) * 128
+    def half_of(k):
+        return h if k < 2 else other
+
+    def blocks_of(k):
+        return [
+            pl.ds(pl.multiple_of(row(k % 2 + 2 * i, half_of(k)), 64), 64) for i in range(2)
+        ]
 
     def to_pair(k):
-        r = pl.ds(pl.multiple_of(rows_of(k), 128), 128)
-        return send(acts.at[1, r], dpre_sib.at[r], sib)
+        return [send(acts.at[1, r], dpre_sib.at[r], sib) for r in blocks_of(k)]
 
     def token_part(k, sd):
-        sd.wait_recv()
-        r = pl.ds(pl.multiple_of(rows_of(k), 128), 128)
+        arrived(sd)
+        mine = jnp.concatenate([acts[1, r] for r in blocks_of(k)], axis=0)
+        his = jnp.concatenate([dpre_sib[r] for r in blocks_of(k)], axis=0)
         for col in range(0, HALF, 512):
             w = win[pl.ds(pl.multiple_of(base + col, 128), 512), :]
-            q = dot(acts[1, r], w, NT) + dot(dpre_sib[r], win_sib[pl.ds(col, 512), :], NT)
+            q = dot(mine, w, NT) + dot(his, win_sib[pl.ds(col, 512), :], NT)
             quad[k, :, :, :, pl.ds(col, 512)] = q.reshape(4, 4, 8, 512)
         out = []
         for j in (2, 1, 3):
@@ -266,51 +271,49 @@
             out.append(send(ysend.at[k, j - 1], yrecv.at[k, j - 1], at(y=yy)))
         return out
 
-    def x_copy(k, xx):
+    def x_copy(k, i):
+        xx = 2 * half_of(k) + i
         j = (xx - x + 4) % 4
-        return pltpu.make_async_remote_copy(
-            src_ref=xsend.at[k], dst_ref=xrecv.at[j - 1],
-            send_sem=xs_sem.at[k], recv_sem=xr_sem.at[j - 1],
+        return xx, pltpu.make_async_remote_copy(
+            src_ref=xsend.at[k, i], dst_ref=xrecv.at[k % 2, j - 1],
+            send_sem=xs_sem.at[k, i], recv_sem=xr_sem.at[k % 2, j - 1],
             device_id=at(x=xx), device_id_type=MESH,
         )
 
-    def x_dest(k):
-        return 2 * (h if k < 2 else other) + k % 2
-
     def y_sum(k, cy):
-        for cp in cy:
-            cp.wait_recv()
+        arrived(cy)
         total = quad[k, :, y].reshape(32, HALF)
         for j in (1, 2, 3):
             total += yrecv[k, j - 1].astype(F32)
-        xx = x_dest(k)
-
-        @pl.when(x == xx)
-        def _():
-            own[...] = total
-
-        @pl.when(x != xx)
-        def _():
-            xsend[k] = total.astype(BF16)
-            x_copy(k, xx).start()
-
-    gathered(1)
+        for i in range(2):
+            xx, cp = x_copy(k, i)
+            piece = total[16 * i : 16 * i + 16]
+
+            @pl.when(x == xx)
+            def _(piece=piece):
+                own[k % 2] = piece
+
+            @pl.when(x != xx)
+            def _(piece=piece, cp=cp):
+                xsend[k, i] = piece.astype(BF16)
+                cp.start()
+
     gathered(2)
     sd = {0: to_pair(0), 1: to_pair(1)}
     cy = {0: token_part(0, sd[0])}
+    finish_sum(3)
     cy[1] = token_part(1, sd[1])
-    finish_sum(3)
+    finish_sum(4)
     pass_on(3)
-    finish_sum(4)
-    y_sum(0, cy[0])
-    y_sum(1, cy[1])
+    pass_on(4)
     gathered(3)
     sd[2] = to_pair(2)
-    pass_on(4)
     cy[2] = token_part(2, sd[2])
     gathered(4)
     sd[3] = to_pair(3)
+    y_sum(0, cy[0])
     cy[3] = token_part(3, sd[3])
+    y_sum(1, cy[1])
 
     def grad_out_tile(i, _):
         col = pl.ds(pl.multiple_of(i * 512, 512), 512)
@@ -331,33 +334,54 @@
     save_i = pltpu.make_async_copy(gwi, gwi_hbm, lsem.at[5])
     save_i.start()
 
-    total = own[...]
-    for j in (1, 2, 3):
+    last = []
+    for core in range(2):
+        total = own[core]
+        for j in (1, 2, 3):
+            pltpu.make_async_remote_copy(
+                src_ref=xsend.at[0, 0], dst_ref=xrecv.at[core, j - 1],
+                send_sem=xs_sem.at[0, 0], recv_sem=xr_sem.at[core, j - 1],
+                device_id=at(x=turn(x, j)), device_id_type=MESH,
+            ).wait_recv()
+            total += xrecv[core, j - 1].astype(F32)
+        fin_send[core] = total.reshape(2, 8, HALF)
+        slot = (c + core) % 2
+        cp = pltpu.make_async_remote_copy(
+            src_ref=fin_send.at[core, other], dst_ref=fin_recv.at[slot],
+            send_sem=fs_sem.at[core], recv_sem=fr_sem.at[slot],
+            device_id=at(h=other, c=core), device_id_type=MESH,
+        )
+        cp.start()
+        last.append(cp)
+    cp = pltpu.make_async_remote_copy(
+        src_ref=fin_send.at[1 - c, h], dst_ref=fin_recv.at[2],
+        send_sem=fs_sem.at[2], recv_sem=fr_sem.at[2],
+        device_id=sib, device_id_type=MESH,
+    )
+    cp.start()
+    last.append(cp)
+    for i in range(3):
         pltpu.make_async_remote_copy(
-            src_ref=xsend.at[0], dst_ref=xrecv.at[j - 1], send_sem=xs_sem.at[0],
-            recv_sem=xr_sem.at[j - 1], device_id=at(x=turn(x, j)), device_id_type=MESH,
+            src_ref=fin_send.at[0, 0], dst_ref=fin_recv.at[i],
+            send_sem=fs_sem.at[i], recv_sem=fr_sem.at[i],
+            device_id=sib, device_id_type=MESH,
         ).wait_recv()
-        total += xrecv[j - 1].astype(F32)
-    fin_send[...] = total.reshape(2, 2, 8, HALF)
-    f1 = send(fin_send.at[c, other], fin_recv.at[0], at(h=other))
-    f2 = send(fin_send.at[1 - c, other], fin_recv.at[1], at(h=other, c=1 - c))
-    f3 = send(fin_send.at[1 - c, h], fin_recv.at[2], sib)
-    f1.wait_recv()
     gt_ref[:, pl.ds(pl.multiple_of(base, 128), HALF)] = (
         fin_send[c, h] + fin_recv[0]
     ).astype(BF16)
-    f2.wait_recv()
-    f3.wait_recv()
     gt_ref[:, pl.ds(pl.multiple_of((1 - c) * HALF, 128), HALF)] = (
         fin_recv[1] + fin_recv[2]
     ).astype(BF16)
 
+    for cp in last:
+        cp.wait_send()
     for k in range(4):
-        xx = x_dest(k)
-
-        @pl.when(x != xx)
-        def _():
-            x_copy(k, xx).wait_send()
+        for i in range(2):
+            xx, cp = x_copy(k, i)
+
+            @pl.when(x != xx)
+            def _(cp=cp):
+                cp.wait_send()
 
     for cp in sent:
         cp.wait_send()
@@ -365,10 +389,33 @@
     save_i.wait()
 
 
+def place(gt, gwi, gwo, gt_out, gwi_out, gwo_out, gt_vm, gwi_vm, gwo_vm, in_sem, out_sem):
+    pieces = []
+    for i in range(4):
+        r = pl.ds(i * (FEAT // 4), FEAT // 4)
+        pieces.append((gwi.at[r], gwi_vm.at[r], gwi_out.at[r]))
+        r = pl.ds(i * (HID // 4), HID // 4)
+        pieces.append((gwo.at[r], gwo_vm.at[r], gwo_out.at[r]))
+    pieces.append((gt, gt_vm, gt_out))
+    into = [
+        pltpu.make_async_copy(src, mid, in_sem.at[i]) for i, (src, mid, _) in enumerate(pieces)
+    ]
+    out = [
+        pltpu.make_async_copy(mid, dst, out_sem.at[i]) for i, (_, mid, dst) in enumerate(pieces)
+    ]
+    for cp in into:
+        cp.start()
+    for a, b in zip(into, out):
+        a.wait()
+        b.start()
+    for cp in out:
+        cp.wait()
+
+
 def shards(tokens, grad_out, w_in, w_out):
     any_ = pl.BlockSpec(memory_space=pl.ANY)
     vm = pltpu.VMEM
-    return pl.pallas_call(
+    grads = pl.pallas_call(
         kernel,
         out_shape=(
             jax.ShapeDtypeStruct((8, FEAT), BF16),
@@ -390,16 +437,18 @@
             vm((4, 4, 4, 8, HALF), F32),
             vm((4, 3, 32, HALF), BF16),
             vm((4, 3, 32, HALF), BF16),
-            vm((4, 32, HALF), BF16),
-            vm((3, 32, HALF), BF16),
-            vm((32, HALF), F32),
+            vm((4, 2, 16, HALF), BF16),
+            vm((2, 3, 16, HALF), BF16),
+            vm((2, 16, HALF), F32),
             vm((2, 2, 8, HALF), F32),
             vm((3, 8, HALF), F32),
             vm((FEAT, HID), BF16),
             vm((HID, FEAT), BF16),
             pltpu.SemaphoreType.DMA((N_SEMS,)),
             pltpu.SemaphoreType.DMA((N_SEMS,)),
-            pltpu.SemaphoreType.DMA((4,)),
+            pltpu.SemaphoreType.DMA((4, 2)),
+            pltpu.SemaphoreType.DMA((2, 3)),
+            pltpu.SemaphoreType.DMA((3,)),
             pltpu.SemaphoreType.DMA((3,)),
             pltpu.SemaphoreType.DMA((6,)),
         ],
@@ -411,6 +460,21 @@
         ),
         name="ffn_backward",
     )(tokens, grad_out, w_in, w_out)
+    return pl.pallas_call(
+        place,
+        out_shape=tuple(jax.ShapeDtypeStruct(g.shape, g.dtype) for g in grads),
+        in_specs=[any_] * 3,
+        out_specs=(any_,) * 3,
+        scratch_shapes=[
+            vm((8, FEAT), BF16),
+            vm((FEAT, HID), BF16),
+            vm((HID, FEAT), BF16),
+            pltpu.SemaphoreType.DMA((9,)),
+            pltpu.SemaphoreType.DMA((9,)),
+        ],
+        compiler_params=pltpu.CompilerParams(vmem_limit_bytes=60 << 20),
+        name="place",
+    )(*grads)
 
 
 def solution(mesh):

time: 94.6 us -> 87.1 us (0.921)
  the two profiles are of different devices: /device:TPU:35 before, /device:TPU:1 now
where the time goes in v3:
time: 87.1 us; the launch traced here: 86.7 us
  Pallas kernels  86 us (99%)
    pallas_call x1, Pallas kernels, shards(): pl.pallas_call(kernel, out_shape=(jax.ShapeDtypeStruct((8, FEAT), BF16),...  81.9 us
    pallas_call x1, Pallas kernels, shards(): pl.pallas_call(place, out_shape=tuple((jax.ShapeDtypeStruct(g.shape, g.dt...  4.14 us

profile of v3, /device:TPU:1, one launch (start us, length us, event | category | flops | bytes accessed | tf_op | source)
XLA Modules:
  0.0 86.7 jit_solution(3304862407042835111)
XLA Ops:
  0.6 81.9 %ffn_backward.1 = (bf16[8,3072]{1,0:T(8,128)(2,1)}, bf16[3072,384]{1,0:T(8,128)(2,1)}, bf16[384,3072]{1,0:T(8,128)(2,1)}) custom-call(bf16[64,3072]{1,0:T(8,128)(2,1)} %tok_hbm.1, bf16[64,3072]{1,0:T(8,128)(2,1)} %dy_hbm.1, bf16[3072,384]{1,0:T(8,128)(2,1)} %win_hbm.1, bf16[384,3072]{1,0:T(8,128)(2,1)} %wout_hbm.1), custom_call_target="tpu_custom_call" | custom-call | flops 6000000000 | bytes 12000000 | tf_op jit(solution)/shard_map/ffn_backward/pallas_call | solution.py:418
  82.5 4.1 %place.1 = (bf16[8,3072]{1,0:T(8,128)(2,1)}, bf16[3072,384]{1,0:T(8,128)(2,1)}, bf16[384,3072]{1,0:T(8,128)(2,1)}) custom-call(bf16[8,3072]{1,0:T(8,128)(2,1)} %get-tuple-element.6.gt, bf16[3072,384]{1,0:T(8,128)(2,1)} %get-tuple-element.7.gwi, bf16[384,3072]{1,0:T(8,128)(2,1)} %get-tuple-element.8.gwo), custom_call_target="tpu_custom_call" | custom-call | tf_op jit(solution)/shard_map/place/pallas_call | solution.py:463

commit v4 on v3

--- a/solution.py
+++ b/solution.py
@@ -17,7 +17,8 @@
 FEAT, HID, TOK = 3072, 384, 512
 HALF = FEAT // 2
 P2O, P2P = 768, 512
-N_SEMS = 128
+N_SEMS = 160
+YF = 1024
 
 
 def gelu_pair(pre, back):
@@ -39,7 +40,8 @@
     gt_ref, gwi_hbm, gwo_hbm,
     both, win, wout, win_sib, part, part16, inbox, acts, dpre_sib,
     quad, ysend, yrecv, xsend, xrecv, own, fin_send, fin_recv, gwi, gwo,
-    ssem, rsem, xs_sem, xr_sem, fs_sem, fr_sem, lsem,
+    zsend, zrecv, wsend, wrecv, ztot,
+    ssem, rsem, xs_sem, xr_sem, fs_sem, fr_sem, zs_sem, zr_sem, ws_sem, wr_sem, lsem,
 ):
     gx, gy, gz = lax.axis_index("gx"), lax.axis_index("gy"), lax.axis_index("gz")
     x, c, y, h, l = gy // 2, gy % 2, gz % 4, gz // 4, gx
@@ -145,12 +147,16 @@
             part[which, pl.ds(pos, n)] = total
             part16[which, pl.ds(pos, n)] = total.astype(BF16)
 
+    late = (turn(y, 2 - 3 * (y % 2)), turn(y, 2 * (y % 2) - 1), turn(y, 1 + y % 2))
+
     chunks = [
         (0, 16, lambda v: row(y, h) + 16 * v),
         (64, 32, lambda v: row(turn(y, 2 * (v // 2) - 1), h) + 32 * (v % 2)),
         (192, 16, lambda v: row(turn(y, 2), h) + 16 * v),
-        (256, 32, lambda v: row(2 * (v // 2), other) + 32 * (v % 2)),
-        (384, 32, lambda v: row(2 * (v // 2) + 1, other) + 32 * (v % 2)),
+        (256, 16, lambda v: row(y, other) + 16 * v),
+        (320, 16, lambda v: row(late[0], other) + 16 * v),
+        (384, 16, lambda v: row(late[1], other) + 16 * v),
+        (448, 16, lambda v: row(late[2], other) + 16 * v),
     ]
 
     def scatter(k):
@@ -226,8 +232,12 @@
     rs[2] = scatter(2)
     arrived(zx)
     pa = to_y(other, 0, 64, 0, P2P)
-    got = [to_sibling(y, other, 0, HALF)]
+    near = to_sibling(y, other, 0, HALF)
+    got = []
     finish_sum(1)
+    near.wait_recv()
+    products(256, [(row(y, other), 64)])
+    rs[3] = scatter(3)
     gathered(0)
     for j in turns:
         arrived(px[j])
@@ -237,11 +247,13 @@
         got.append(to_sibling(turn(y, -j), other, 0, P2P))
     finish_sum(2)
     pass_on(1)
+    finish_sum(3)
     arrived(got)
-    products(256, [(row(b, other), 64) for b in (0, 2, 1, 3)])
-    rs[3] = scatter(3)
-    rs[4] = scatter(4)
+    products(320, [(row(b, other), 64) for b in late])
+    for k in (4, 5, 6):
+        rs[k] = scatter(k)
     pass_on(2)
+    pass_on(3)
     gathered(1)
     ws.wait_recv()
 
@@ -265,51 +277,108 @@
             q = dot(mine, w, NT) + dot(his, win_sib[pl.ds(col, 512), :], NT)
             quad[k, :, :, :, pl.ds(col, 512)] = q.reshape(4, 4, 8, 512)
         out = []
+        n = cols_of(k)
         for j in (2, 1, 3):
             yy = turn(y, j)
-            ysend[k, j - 1] = quad[k, :, yy].reshape(32, HALF).astype(BF16)
-            out.append(send(ysend.at[k, j - 1], yrecv.at[k, j - 1], at(y=yy)))
+            ysend[k, j - 1, :, 0:n] = quad[k, :, yy, :, 0:n].reshape(32, n).astype(BF16)
+            out.append(send(
+                ysend.at[k, j - 1, :, pl.ds(0, n)], yrecv.at[k, j - 1, :, pl.ds(0, n)], at(y=yy)
+            ))
+        if k >= 2:
+            for i in range(2):
+                xx, cp = z_copy(k, i)
+
+                @pl.when(x != xx)
+                def _(i=i, cp=cp):
+                    zsend[k - 2, i] = (
+                        quad[k, 2 * i : 2 * i + 2, :, :, YF:HALF].reshape(64, HALF - YF).astype(BF16)
+                    )
+                    cp.start()
         return out
+
+    def z_copy(k, i):
+        xx = 2 * half_of(k) + i
+        j = (xx - x + 4) % 4
+        return xx, pltpu.make_async_remote_copy(
+            src_ref=zsend.at[k - 2, i], dst_ref=zrecv.at[k - 2, j - 1],
+            send_sem=zs_sem.at[k - 2, i], recv_sem=zr_sem.at[k - 2, j - 1],
+            device_id=at(x=xx), device_id_type=MESH,
+        )
+
+    def w_copy(k, j):
+        return pltpu.make_async_remote_copy(
+            src_ref=wsend.at[k - 2, j - 1], dst_ref=wrecv.at[k - 2, j - 1],
+            send_sem=ws_sem.at[k - 2, j - 1], recv_sem=wr_sem.at[k - 2, j - 1],
+            device_id=at(y=turn(y, j)), device_id_type=MESH,
+        )
+
+    def x_sum(k):
+        @pl.when(x // 2 == other)
+        def _():
+            total = quad[k, pl.ds(2 * (x % 2), 2), :, :, YF:HALF]
+            for j in (1, 2, 3):
+                pltpu.make_async_remote_copy(
+                    src_ref=zsend.at[0, 0], dst_ref=zrecv.at[k - 2, j - 1],
+                    send_sem=zs_sem.at[0, 0], recv_sem=zr_sem.at[k - 2, j - 1],
+                    device_id=at(x=turn(x, j)), device_id_type=MESH,
+                ).wait_recv()
+                total += zrecv[k - 2, j - 1].astype(F32).reshape(2, 4, 8, HALF - YF)
+            ztot[...] = total
+            for j in (2, 1, 3):
+                wsend[k - 2, j - 1] = (
+                    ztot[:, turn(y, j)].reshape(16, HALF - YF).astype(BF16)
+                )
+                w_copy(k, j).start()
+            own[k - 2, :, YF:HALF] = ztot[:, y].reshape(16, HALF - YF)
+
+    def cols_of(k):
+        return HALF if k < 2 else YF
 
     def x_copy(k, i):
         xx = 2 * half_of(k) + i
         j = (xx - x + 4) % 4
         return xx, pltpu.make_async_remote_copy(
-            src_ref=xsend.at[k, i], dst_ref=xrecv.at[k % 2, j - 1],
+            src_ref=xsend.at[k, i, :, pl.ds(0, cols_of(k))],
+            dst_ref=xrecv.at[k % 2, j - 1, :, pl.ds(0, cols_of(k))],
             send_sem=xs_sem.at[k, i], recv_sem=xr_sem.at[k % 2, j - 1],
             device_id=at(x=xx), device_id_type=MESH,
         )
 
     def y_sum(k, cy):
         arrived(cy)
-        total = quad[k, :, y].reshape(32, HALF)
+        n = cols_of(k)
+        total = quad[k, :, y, :, 0:n].reshape(32, n)
         for j in (1, 2, 3):
-            total += yrecv[k, j - 1].astype(F32)
+            total += yrecv[k, j - 1, :, 0:n].astype(F32)
         for i in range(2):
             xx, cp = x_copy(k, i)
             piece = total[16 * i : 16 * i + 16]
 
             @pl.when(x == xx)
             def _(piece=piece):
-                own[k % 2] = piece
+                own[k % 2, :, 0:n] = piece
 
             @pl.when(x != xx)
             def _(piece=piece, cp=cp):
-                xsend[k, i] = piece.astype(BF16)
+                xsend[k, i, :, 0:n] = piece.astype(BF16)
                 cp.start()
 
     gathered(2)
     sd = {0: to_pair(0), 1: to_pair(1)}
     cy = {0: token_part(0, sd[0])}
-    finish_sum(3)
+    finish_sum(4)
+    finish_sum(5)
     cy[1] = token_part(1, sd[1])
-    finish_sum(4)
-    pass_on(3)
+    finish_sum(6)
     pass_on(4)
+    pass_on(5)
+    pass_on(6)
     gathered(3)
+    gathered(4)
+    gathered(5)
     sd[2] = to_pair(2)
     cy[2] = token_part(2, sd[2])
-    gathered(4)
+    gathered(6)
     sd[3] = to_pair(3)
     y_sum(0, cy[0])
     cy[3] = token_part(3, sd[3])
@@ -329,22 +398,40 @@
     save_o = pltpu.make_async_copy(gwo, gwo_hbm, lsem.at[4])
     save_o.start()
     y_sum(2, cy[2])
+    x_sum(2)
     y_sum(3, cy[3])
+    x_sum(3)
     lax.fori_loop(0, FEAT // 512, grad_in_tile, 0)
     save_i = pltpu.make_async_copy(gwi, gwi_hbm, lsem.at[5])
     save_i.start()
 
     last = []
     for core in range(2):
-        total = own[core]
-        for j in (1, 2, 3):
-            pltpu.make_async_remote_copy(
-                src_ref=xsend.at[0, 0], dst_ref=xrecv.at[core, j - 1],
-                send_sem=xs_sem.at[0, 0], recv_sem=xr_sem.at[core, j - 1],
-                device_id=at(x=turn(x, j)), device_id_type=MESH,
-            ).wait_recv()
-            total += xrecv[core, j - 1].astype(F32)
-        fin_send[core] = total.reshape(2, 8, HALF)
+        def from_x(core, n):
+            total = own[core, :, 0:n]
+            for j in (1, 2, 3):
+                pltpu.make_async_remote_copy(
+                    src_ref=xsend.at[0, 0, :, pl.ds(0, n)],
+                    dst_ref=xrecv.at[core, j - 1, :, pl.ds(0, n)],
+                    send_sem=xs_sem.at[0, 0], recv_sem=xr_sem.at[core, j - 1],
+                    device_id=at(x=turn(x, j)), device_id_type=MESH,
+                ).wait_recv()
+                total += xrecv[core, j - 1, :, 0:n].astype(F32)
+            fin_send[core, :, :, 0:n] = total.reshape(2, 8, n)
+
+        @pl.when(x // 2 == h)
+        def _(core=core):
+            from_x(core, HALF)
+
+        @pl.when(x // 2 == other)
+        def _(core=core):
+            from_x(core, YF)
+            total = own[core, :, YF:HALF]
+            for j in (1, 2, 3):
+                w_copy(core + 2, j).wait_recv()
+                total += wrecv[core, j - 1].astype(F32)
+            fin_send[core, :, :, YF:HALF] = total.reshape(2, 8, HALF - YF)
+
         slot = (c + core) % 2
         cp = pltpu.make_async_remote_copy(
             src_ref=fin_send.at[core, other], dst_ref=fin_recv.at[slot],
@@ -383,6 +470,19 @@
             def _(cp=cp):
                 cp.wait_send()
 
+    for k in (2, 3):
+        for i in range(2):
+            xx, cp = z_copy(k, i)
+
+            @pl.when(x != xx)
+            def _(cp=cp):
+                cp.wait_send()
+
+        @pl.when(x // 2 == other)
+        def _(k=k):
+            for j in (1, 2, 3):
+                w_copy(k, j).wait_send()
+
     for cp in sent:
         cp.wait_send()
     save_o.wait()
@@ -431,7 +531,7 @@
             vm((HALF, HID), BF16),
             vm((2, TOK, HID), F32),
             vm((2, TOK, HID), BF16),
-            vm((5, 3, 2, 32, HID), BF16),
+            vm((7, 3, 2, 32, HID), BF16),
             vm((2, TOK, HID), BF16),
             vm((TOK, HID), BF16),
             vm((4, 4, 4, 8, HALF), F32),
@@ -444,12 +544,21 @@
             vm((3, 8, HALF), F32),
             vm((FEAT, HID), BF16),
             vm((HID, FEAT), BF16),
+            vm((2, 2, 64, HALF - YF), BF16),
+            vm((2, 3, 64, HALF - YF), BF16),
+            vm((2, 3, 16, HALF - YF), BF16),
+            vm((2, 3, 16, HALF - YF), BF16),
+            vm((2, 4, 8, HALF - YF), F32),
             pltpu.SemaphoreType.DMA((N_SEMS,)),
             pltpu.SemaphoreType.DMA((N_SEMS,)),
             pltpu.SemaphoreType.DMA((4, 2)),
             pltpu.SemaphoreType.DMA((2, 3)),
             pltpu.SemaphoreType.DMA((3,)),
             pltpu.SemaphoreType.DMA((3,)),
+            pltpu.SemaphoreType.DMA((2, 2)),
+            pltpu.SemaphoreType.DMA((2, 3)),
+            pltpu.SemaphoreType.DMA((2, 3)),
+            pltpu.SemaphoreType.DMA((2, 3)),
             pltpu.SemaphoreType.DMA((6,)),
         ],
         compiler_params=pltpu.CompilerParams(

time: 87.1 us -> 84.5 us (0.970)
  Pallas kernels: 86 us -> 83.8 us
    pallas_call x1, Pallas kernels: 81.9 us -> 79.7 us  [shards(): pl.pallas_call(kernel, out_shape=(jax.ShapeDtypeStruct((8, FEAT), BF16),...]
where the time goes in v4:
time: 84.5 us; the launch traced here: 84.4 us
  Pallas kernels  83.8 us (99%)
    pallas_call x1, Pallas kernels, shards(): pl.pallas_call(kernel, out_shape=(jax.ShapeDtypeStruct((8, FEAT), BF16),...  79.7 us
    pallas_call x1, Pallas kernels, shards(): pl.pallas_call(place, out_shape=tuple((jax.ShapeDtypeStruct(g.shape, g.dt...  4.14 us

profile of v4, /device:TPU:1, one launch (start us, length us, event | category | flops | bytes accessed | tf_op | source)
XLA Modules:
  0.0 84.4 jit_solution(180750737590189165)
XLA Ops:
  0.6 79.7 %ffn_backward.1 = (bf16[8,3072]{1,0:T(8,128)(2,1)}, bf16[3072,384]{1,0:T(8,128)(2,1)}, bf16[384,3072]{1,0:T(8,128)(2,1)}) custom-call(bf16[64,3072]{1,0:T(8,128)(2,1)} %tok_hbm.1, bf16[64,3072]{1,0:T(8,128)(2,1)} %dy_hbm.1, bf16[3072,384]{1,0:T(8,128)(2,1)} %win_hbm.1, bf16[384,3072]{1,0:T(8,128)(2,1)} %wout_hbm.1), custom_call_target="tpu_custom_call" | custom-call | flops 6000000000 | bytes 12000000 | tf_op jit(solution)/shard_map/ffn_backward/pallas_call | solution.py:518
  80.3 4.1 %place.1 = (bf16[8,3072]{1,0:T(8,128)(2,1)}, bf16[3072,384]{1,0:T(8,128)(2,1)}, bf16[384,3072]{1,0:T(8,128)(2,1)}) custom-call(bf16[8,3072]{1,0:T(8,128)(2,1)} %get-tuple-element.6.gt, bf16[3072,384]{1,0:T(8,128)(2,1)} %get-tuple-element.7.gwi, bf16[384,3072]{1,0:T(8,128)(2,1)} %get-tuple-element.8.gwo), custom_call_target="tpu_custom_call" | custom-call | tf_op jit(solution)/shard_map/place/pallas_call | solution.py:572

commit v5 on v4

--- a/solution.py
+++ b/solution.py
@@ -368,8 +368,8 @@
     cy = {0: token_part(0, sd[0])}
     finish_sum(4)
     finish_sum(5)
+    finish_sum(6)
     cy[1] = token_part(1, sd[1])
-    finish_sum(6)
     pass_on(4)
     pass_on(5)
     pass_on(6)
@@ -380,8 +380,8 @@
     cy[2] = token_part(2, sd[2])
     gathered(6)
     sd[3] = to_pair(3)
+    cy[3] = token_part(3, sd[3])
     y_sum(0, cy[0])
-    cy[3] = token_part(3, sd[3])
     y_sum(1, cy[1])
 
     def grad_out_tile(i, _):

time: 84.5 us -> 83.7 us (level)
  no operation moved by 1% of the time
where the time goes in v5:
time: 83.7 us; the launch traced here: 83.6 us
  Pallas kernels  83 us (99%)
    pallas_call x1, Pallas kernels, shards(): pl.pallas_call(kernel, out_shape=(jax.ShapeDtypeStruct((8, FEAT), BF16),...  78.8 us
    pallas_call x1, Pallas kernels, shards(): pl.pallas_call(place, out_shape=tuple((jax.ShapeDtypeStruct(g.shape, g.dt...  4.14 us

profile of v5, /device:TPU:1, one launch (start us, length us, event | category | flops | bytes accessed | tf_op | source)
XLA Modules:
  0.0 83.6 jit_solution(13159097032969335551)
XLA Ops:
  0.6 78.8 %ffn_backward.1 = (bf16[8,3072]{1,0:T(8,128)(2,1)}, bf16[3072,384]{1,0:T(8,128)(2,1)}, bf16[384,3072]{1,0:T(8,128)(2,1)}) custom-call(bf16[64,3072]{1,0:T(8,128)(2,1)} %tok_hbm.1, bf16[64,3072]{1,0:T(8,128)(2,1)} %dy_hbm.1, bf16[3072,384]{1,0:T(8,128)(2,1)} %win_hbm.1, bf16[384,3072]{1,0:T(8,128)(2,1)} %wout_hbm.1), custom_call_target="tpu_custom_call" | custom-call | flops 6000000000 | bytes 12000000 | tf_op jit(solution)/shard_map/ffn_backward/pallas_call | solution.py:518
  79.5 4.1 %place.1 = (bf16[8,3072]{1,0:T(8,128)(2,1)}, bf16[3072,384]{1,0:T(8,128)(2,1)}, bf16[384,3072]{1,0:T(8,128)(2,1)}) custom-call(bf16[8,3072]{1,0:T(8,128)(2,1)} %get-tuple-element.6.gt, bf16[3072,384]{1,0:T(8,128)(2,1)} %get-tuple-element.7.gwi, bf16[384,3072]{1,0:T(8,128)(2,1)} %get-tuple-element.8.gwo), custom_call_target="tpu_custom_call" | custom-call | tf_op jit(solution)/shard_map/place/pallas_call | solution.py:572

commit v6 on v5

--- a/solution.py
+++ b/solution.py
@@ -19,6 +19,7 @@
 P2O, P2P = 768, 512
 N_SEMS = 160
 YF = 1024
+DIRECT = (2, 3, 4, 5, 6)
 
 
 def gelu_pair(pre, back):
@@ -186,6 +187,8 @@
         acts[1, q] = dpre
         ref = acts.at[:, q]
         ag[k] = [send(ref, ref, at(l=l2)), send(ref, ref, at(l=l1))]
+        if k in DIRECT:
+            ag[k].append(send(ref, ref, at(l=l3)))
 
     def pass_on(k):
         ag[k][0].wait_recv()
@@ -195,6 +198,8 @@
     def gathered(k):
         ag[k][1].wait_recv()
         ag[k][2].wait_recv()
+        if k in DIRECT:
+            ag[k][0].wait_recv()
 
     rs, ag = {}, {}
     yb = to_y(h, strip, 16, P2O, HALF - P2O)
@@ -252,8 +257,6 @@
     products(320, [(row(b, other), 64) for b in late])
     for k in (4, 5, 6):
         rs[k] = scatter(k)
-    pass_on(2)
-    pass_on(3)
     gathered(1)
     ws.wait_recv()
 
@@ -370,9 +373,6 @@
     finish_sum(5)
     finish_sum(6)
     cy[1] = token_part(1, sd[1])
-    pass_on(4)
-    pass_on(5)
-    pass_on(6)
     gathered(3)
     gathered(4)
     gathered(5)

time: 83.7 us -> 81.2 us (0.970)
  Pallas kernels: 83 us -> 79.7 us
    pallas_call x1, Pallas kernels: 78.8 us -> 75.5 us  [shards(): pl.pallas_call(kernel, out_shape=(jax.ShapeDtypeStruct((8, FEAT), BF16),...]
where the time goes in v6:
time: 81.2 us; the launch traced here: 80.3 us
  Pallas kernels  79.7 us (98%)
    pallas_call x1, Pallas kernels, shards(): pl.pallas_call(kernel, out_shape=(jax.ShapeDtypeStruct((8, FEAT), BF16),...  75.5 us
    pallas_call x1, Pallas kernels, shards(): pl.pallas_call(place, out_shape=tuple((jax.ShapeDtypeStruct(g.shape, g.dt...  4.14 us

profile of v6, /device:TPU:1, one launch (start us, length us, event | category | flops | bytes accessed | tf_op | source)
XLA Modules:
  0.0 80.3 jit_solution(5474234568041680621)
XLA Ops:
  0.6 75.5 %ffn_backward.1 = (bf16[8,3072]{1,0:T(8,128)(2,1)}, bf16[3072,384]{1,0:T(8,128)(2,1)}, bf16[384,3072]{1,0:T(8,128)(2,1)}) custom-call(bf16[64,3072]{1,0:T(8,128)(2,1)} %tok_hbm.1, bf16[64,3072]{1,0:T(8,128)(2,1)} %dy_hbm.1, bf16[3072,384]{1,0:T(8,128)(2,1)} %win_hbm.1, bf16[384,3072]{1,0:T(8,128)(2,1)} %wout_hbm.1), custom_call_target="tpu_custom_call" | custom-call | flops 6000000000 | bytes 12000000 | tf_op jit(solution)/shard_map/ffn_backward/pallas_call | solution.py:518
  76.2 4.1 %place.1 = (bf16[8,3072]{1,0:T(8,128)(2,1)}, bf16[3072,384]{1,0:T(8,128)(2,1)}, bf16[384,3072]{1,0:T(8,128)(2,1)}) custom-call(bf16[8,3072]{1,0:T(8,128)(2,1)} %get-tuple-element.6.gt, bf16[3072,384]{1,0:T(8,128)(2,1)} %get-tuple-element.7.gwi, bf16[384,3072]{1,0:T(8,128)(2,1)} %get-tuple-element.8.gwo), custom_call_target="tpu_custom_call" | custom-call | tf_op jit(solution)/shard_map/place/pallas_call | solution.py:572
